TPU v7x, 32 devices: a whole 2x2x4 slice. The times are simulated.
32 devices in a mesh: parts: 2 (over x), row: 16 (over z, y, core).
Axes of the slice: x: 2, y: 2, z: 4, core: 2. Of those that a mesh axis runs over, the one named last changes fastest.
Arguments:
- vectors: bfloat16 [32768, 128], P(('parts', 'row')), parts along dimension 0, may hold values from -6 to 6
- tiles: bfloat16 [8192, 128, 128], P(('parts', 'row')), parts along dimension 0, may hold values from -0.046875 to 0.046875
- tile_cols: int32 [8192], P(('parts', 'row')), parts along dimension 0, may hold values from -1 to 127, as said below
- ritz: bfloat16 [256, 128], P('parts'), parts along dimension 0, may hold values from -0.5 to 0.5
Outputs:
- rotated: bfloat16 [32768, 128], P(('parts', 'row')), parts along dimension 0
- gram: float32 [256, 128], P('parts'), parts along dimension 0
There are 2 independent parts, one for each index of `parts`. A program takes and returns all parts, laid end to end along the dimension named above; each array names one. Nothing has to cross between parts.
Inputs may be any that keep to these rules, and one draw needn't show every extreme that they name: `tile_cols`: entry t * 32 + j belongs to tile row t; the live slots of a tile row come first and the rest are -1; every tile row has 8 or more live slots and some tile row has all 32; a live column lies between (t // 8 - 2) * 8 and (t // 8 + 3) * 8 - 1.
All inputs are finite; a program needn't handle non-finite values.
Results may differ from a plain program's by a relative error of at most 0.0058.
Values may be sent and summed in bfloat16 or wider, within the bound.
A program may use at most 64 MiB of HBM per device.

v0:
```python
import jax
import jax.numpy as jnp
from jax import lax
from jax.sharding import PartitionSpec as P

REACH = 2
DEG = 4


def shifted(block, axis, distance):
    devices = range(lax.axis_size(axis))
    route = [(i - distance, i) for i in devices if i - distance in devices]
    return lax.ppermute(block, axis, route)


def body(vectors, tiles, tile_cols, ritz):
    rows_here = vectors.shape[0]
    tile = tiles.shape[1]
    width = vectors.shape[1]
    tile_rows = rows_here // tile
    per_row = tiles.shape[0] // tile_rows
    first_col = (lax.axis_index("row") - REACH) * tile_rows
    live = tile_cols >= 0
    position = jnp.where(live, tile_cols - first_col, 0)
    grouped = tiles.reshape(tile_rows, per_row, tile, tile)

    def apply_operator(current):
        lower = [shifted(current, "row", dist) for dist in range(REACH, 0, -1)]
        upper = [shifted(current, "row", -dist) for dist in range(1, REACH + 1)]
        extended = jnp.concatenate(lower + [current] + upper, 0)
        blocks = extended.reshape(-1, tile, width)
        picked = blocks[position]
        picked = jnp.where(live[:, None, None], picked, jnp.zeros_like(picked))
        picked = picked.reshape(tile_rows, per_row, tile, width)
        result = jnp.einsum("rjab,rjbk->rak", grouped, picked, preferred_element_type=jnp.float32)
        return result.reshape(rows_here, width)

    previous = vectors
    current = apply_operator(vectors).astype(jnp.bfloat16)
    for step in range(DEG - 1):
        nxt = 2.0 * apply_operator(current) - previous.astype(jnp.float32)
        previous, current = (current, nxt.astype(jnp.bfloat16))
    partial_gram = jnp.einsum("nk,nl->kl", current, current, preferred_element_type=jnp.float32)
    total = lax.psum(partial_gram, "row")
    gram = total * float(rows_here * lax.axis_size("row")) ** (-0.5)
    rotated = jnp.dot(current, ritz, preferred_element_type=jnp.float32).astype(jnp.bfloat16)
    return (rotated, gram)


def solution(mesh):
    return jax.shard_map(
        body,
        mesh=mesh,
        in_specs=(
            P(("parts", "row"), None),
            P(("parts", "row"), None, None),
            P(("parts", "row")),
            P("parts", None),
        ),
        out_specs=(P(("parts", "row"), None), P("parts", None)),
        check_vma=False,
    )
```

profile of v0, /device:TPU:0, one launch (start us, length us, event | category | flops | bytes accessed | tf_op | source)
XLA Modules:
  0.0 255.5 jit_solution(13914823277958229322)
XLA Ops:
  7.2 0.0 copy-start
  7.2 0.0 all-reduce.2.cloned.1.call-start
  7.2 1.3 collective-permute-start.3
  8.5 1.3 collective-permute-start.2
  9.8 3.1 %collective-permute-start.1 = (bf16[1024,128]{1,0:T(8,128)(2,1)}, bf16[1024,128]{1,0:T(8,128)(2,1)S(1)}, u32[]{:S(2)}, u32[]{:S(2)}) collective-permute-start(bf16[1024,128]{1,0:T(8,128)(2,1)} %param.4), channel_id=1, source_target_pairs={{0,1},{1,2},{2,3},{3,4},{4,5},{5,6},{6,7},{7,8},{8,9},{9,10},{10,1... | collective-permute-start | bytes 786440 | tf_op jit(solution)/shard_map/ppermute | solution.py:13
  12.9 5.5 %collective-permute-start = (bf16[1024,128]{1,0:T(8,128)(2,1)}, bf16[1024,128]{1,0:T(8,128)(2,1)S(1)}, u32[]{:S(2)}, u32[]{:S(2)}) collective-permute-start(bf16[1024,128]{1,0:T(8,128)(2,1)} %param.4), channel_id=1, source_target_pairs={{0,2},{1,3},{2,4},{3,5},{4,6},{5,7},{6,8},{7,9},{8,10},{9,11},{10,... | collective-permute-start | bytes 786440 | tf_op jit(solution)/shard_map/ppermute | solution.py:13
  18.4 0.7 compare_select_fusion
  19.1 0.7 broadcast_compare_fusion
  19.8 0.1 broadcast_in_dim.31
  19.9 7.5 %collective-permute-done = bf16[1024,128]{1,0:T(8,128)(2,1)S(1)} collective-permute-done((bf16[1024,128]{1,0:T(8,128)(2,1)}, bf16[1024,128]{1,0:T(8,128)(2,1)S(1)}, u32[]{:S(2)}, u32[]{:S(2)}) %collective-permute-start) | collective-permute-done | bytes 262176 | tf_op jit(solution)/shard_map/ppermute | solution.py:13
  27.4 0.0 collective-permute-done.1
  27.5 1.0 constant_dynamic-update-slice_fusion.2
  28.5 0.0 collective-permute-done.2
  28.5 0.0 collective-permute-done.3
  28.6 8.6 %gather_fusion = bf16[256,128,128]{2,1,0:T(8,128)(2,1)} fusion(bf16[40,128,128]{2,1,0:T(8,128)(2,1)S(1)} %bitcast.59, s32[1024]{0:T(1024)S(1)} %pad_clamp_fusion), kind=kCustom, calls=%fused_computation | custom fusion | bytes 16778240 | tf_op jit(solution)/shard_map/gather | solution.py:32
  37.1 8.2 %fusion.28 = bf16[8,128,128]{1,2,0:T(8,128)(2,1)S(1)} fusion(bf16[8,32,128,128]{3,2,1,0:T(8,128)(2,1)} %bitcast.72, bf16[8,32,128,128]{3,2,1,0:T(8,128)(2,1)} %bitcast.64, pred[8,32]{1,0:T(8,128)(4,1)S(1)} %broadcast_in_dim.31), kind=kOutput, calls=%fused_computation.25 | convolution fusion | flops 1078067200 | bytes 17039616 | tf_op jit(solution)/shard_map/rjab,rjbk->rak/dot_general | solution.py:35
  45.3 4.2 %collective-permute-start.4 = (bf16[1024,128]{1,0:T(8,128)(2,1)S(1)}, bf16[1024,128]{1,0:T(8,128)(2,1)S(1)}, u32[]{:S(2)}, u32[]{:S(2)}) collective-permute-start(bf16[1024,128]{1,0:T(8,128)(2,1)S(1)} %bitcast.67), channel_id=1, source_target_pairs={{0,2},{1,3},{2,4},{3,5},{4,6},{5,7},{6,8},{7,9},{8,10},{9,11},{10,... | collective-permute-start | bytes 786440 | tf_op jit(solution)/shard_map/ppermute | solution.py:13
  49.5 4.2 %collective-permute-start.5 = (bf16[1024,128]{1,0:T(8,128)(2,1)S(1)}, bf16[1024,128]{1,0:T(8,128)(2,1)S(1)}, u32[]{:S(2)}, u32[]{:S(2)}) collective-permute-start(bf16[1024,128]{1,0:T(8,128)(2,1)S(1)} %bitcast.68), channel_id=1, source_target_pairs={{0,1},{1,2},{2,3},{3,4},{4,5},{5,6},{6,7},{7,8},{8,9},{9,10},{10,1... | collective-permute-start | bytes 786440 | tf_op jit(solution)/shard_map/ppermute | solution.py:13
  53.8 1.3 collective-permute-start.7
  55.1 1.3 collective-permute-start.6
  56.4 0.0 collective-permute-done.4
  56.4 0.0 collective-permute-done.5
  56.5 2.0 collective-permute-done.6
  58.5 5.3 %collective-permute-done.7 = bf16[1024,128]{1,0:T(8,128)(2,1)S(1)} collective-permute-done((bf16[1024,128]{1,0:T(8,128)(2,1)S(1)}, bf16[1024,128]{1,0:T(8,128)(2,1)S(1)}, u32[]{:S(2)}, u32[]{:S(2)}) %collective-permute-start.7) | collective-permute-done | bytes 262176 | tf_op jit(solution)/shard_map/ppermute | solution.py:13
  63.9 8.6 %gather_fusion.1 = bf16[256,128,128]{2,1,0:T(8,128)(2,1)} fusion(bf16[40,128,128]{2,1,0:T(8,128)(2,1)S(1)} %bitcast.60, s32[1024]{0:T(1024)S(1)} %pad_clamp_fusion), kind=kCustom, calls=%fused_computation.1 | custom fusion | bytes 16778240 | tf_op jit(solution)/shard_map/gather | solution.py:32
  72.5 0.0 copy-start.1
  72.5 8.2 %fusion.37 = f32[8,128,128]{1,2,0:T(8,128)S(1)} fusion(bf16[8,32,128,128]{3,2,1,0:T(8,128)(2,1)} %bitcast.73, bf16[8,32,128,128]{3,2,1,0:T(8,128)(2,1)} %bitcast.65, pred[8,32]{1,0:T(8,128)(4,1)S(1)} %broadcast_in_dim.31), kind=kOutput, calls=%fused_computation.28 | convolution fusion | flops 1078067200 | bytes 17301760 | tf_op jit(solution)/shard_map/rjab,rjbk->rak/dot_general | solution.py:35
  80.7 0.0 copy-done.1
  80.7 0.1 fusion.42
  80.8 8.0 %collective-permute-start.8 = (bf16[1024,128]{1,0:T(8,128)(2,1)S(1)}, bf16[1024,128]{1,0:T(8,128)(2,1)S(1)}, u32[]{:S(2)}, u32[]{:S(2)}) collective-permute-start(bf16[1024,128]{1,0:T(8,128)(2,1)S(1)} %fusion.42), channel_id=1, source_target_pairs={{0,2},{1,3},{2,4},{3,5},{4,6},{5,7},{6,8},{7,9},{8,10},{9,11},{10,... | collective-permute-start | bytes 786440 | tf_op jit(solution)/shard_map/ppermute | solution.py:13
  88.8 1.3 collective-permute-start.9
  90.1 1.3 collective-permute-start.11
  91.4 1.5 collective-permute-start.10
  92.9 1.9 collective-permute-done.8
  94.8 0.0 collective-permute-done.9
  94.9 0.1 collective-permute-done.10
  95.1 6.5 %collective-permute-done.11 = bf16[1024,128]{1,0:T(8,128)(2,1)S(1)} collective-permute-done((bf16[1024,128]{1,0:T(8,128)(2,1)S(1)}, bf16[1024,128]{1,0:T(8,128)(2,1)S(1)}, u32[]{:S(2)}, u32[]{:S(2)}) %collective-permute-start.11) | collective-permute-done | bytes 262176 | tf_op jit(solution)/shard_map/ppermute | solution.py:13
  101.7 8.6 %gather_fusion.2 = bf16[256,128,128]{2,1,0:T(8,128)(2,1)} fusion(bf16[40,128,128]{2,1,0:T(8,128)(2,1)S(1)} %bitcast.61, s32[1024]{0:T(1024)S(1)} %pad_clamp_fusion), kind=kCustom, calls=%fused_computation.2 | custom fusion | bytes 16778240 | tf_op jit(solution)/shard_map/gather | solution.py:32
  110.2 8.2 %fusion.34 = f32[8,128,128]{1,2,0:T(8,128)S(1)} fusion(bf16[8,32,128,128]{3,2,1,0:T(8,128)(2,1)} %bitcast.74, bf16[8,32,128,128]{3,2,1,0:T(8,128)(2,1)} %bitcast.66, pred[8,32]{1,0:T(8,128)(4,1)S(1)} %broadcast_in_dim.31), kind=kOutput, calls=%fused_computation.27 | convolution fusion | flops 1078067200 | bytes 17301760 | tf_op jit(solution)/shard_map/rjab,rjbk->rak/dot_general | solution.py:35
  118.4 0.1 fusion.41
  118.5 4.9 %collective-permute-start.12 = (bf16[1024,128]{1,0:T(8,128)(2,1)S(1)}, bf16[1024,128]{1,0:T(8,128)(2,1)S(1)}, u32[]{:S(2)}, u32[]{:S(2)}) collective-permute-start(bf16[1024,128]{1,0:T(8,128)(2,1)S(1)} %fusion.41), channel_id=1, source_target_pairs={{0,2},{1,3},{2,4},{3,5},{4,6},{5,7},{6,8},{7,9},{8,10},{9,11},{10,... | collective-permute-start | bytes 786440 | tf_op jit(solution)/shard_map/ppermute | solution.py:13
  123.5 4.5 %collective-permute-start.13 = (bf16[1024,128]{1,0:T(8,128)(2,1)S(1)}, bf16[1024,128]{1,0:T(8,128)(2,1)S(1)}, u32[]{:S(2)}, u32[]{:S(2)}) collective-permute-start(bf16[1024,128]{1,0:T(8,128)(2,1)S(1)} %fusion.41), channel_id=1, source_target_pairs={{0,1},{1,2},{2,3},{3,4},{4,5},{5,6},{6,7},{7,8},{8,9},{9,10},{10,1... | collective-permute-start | bytes 786440 | tf_op jit(solution)/shard_map/ppermute | solution.py:13
  128.0 1.3 collective-permute-start.15
  129.3 1.3 collective-permute-start.14
  130.6 0.0 collective-permute-done.12
  130.6 0.0 collective-permute-done.13
  130.7 2.0 collective-permute-done.14
  132.8 5.8 %collective-permute-done.15 = bf16[1024,128]{1,0:T(8,128)(2,1)S(1)} collective-permute-done((bf16[1024,128]{1,0:T(8,128)(2,1)S(1)}, bf16[1024,128]{1,0:T(8,128)(2,1)S(1)}, u32[]{:S(2)}, u32[]{:S(2)}) %collective-permute-start.15) | collective-permute-done | bytes 262176 | tf_op jit(solution)/shard_map/ppermute | solution.py:13
  138.6 8.6 %gather_fusion.3 = bf16[256,128,128]{2,1,0:T(8,128)(2,1)} fusion(bf16[40,128,128]{2,1,0:T(8,128)(2,1)S(1)} %bitcast.62, s32[1024]{0:T(1024)S(1)} %pad_clamp_fusion), kind=kCustom, calls=%fused_computation.3 | custom fusion | bytes 16778240 | tf_op jit(solution)/shard_map/gather | solution.py:32
  147.2 8.2 %fusion.31 = f32[8,128,128]{1,2,0:T(8,128)S(1)} fusion(bf16[8,32,128,128]{3,2,1,0:T(8,128)(2,1)} %bitcast.75, bf16[8,32,128,128]{3,2,1,0:T(8,128)(2,1)} %bitcast.63, pred[8,32]{1,0:T(8,128)(4,1)S(1)} %broadcast_in_dim.31), kind=kOutput, calls=%fused_computation.26 | convolution fusion | flops 1078067200 | bytes 17301760 | tf_op jit(solution)/shard_map/rjab,rjbk->rak/dot_general | solution.py:35
  155.4 0.1 fusion.40
  155.4 0.9 fusion.47
  156.3 0.0 all-reduce.2.cloned.1.call-update
  156.4 0.0 copy-done
  156.4 0.9 convolution_convert_fusion
  157.3 89.9 %all-reduce.2.cloned.1.call-done = f32[128,128]{1,0:T(8,128)} async-done(((f32[128,128]{1,0:T(8,128)}), f32[128,128]{1,0:T(8,128)}) %all-reduce.2.cloned.1.call-update) | async-done | bytes 65552 | tf_op jit(solution)/shard_map/psum | solution.py:44
  247.2 1.5 broadcast_multiply_fusion
  (20 shorter events, 0.6 us)
Async XLA Ops:
  7.2 149.2 %copy-start = (bf16[128,128]{1,0:T(8,128)(2,1)S(1)}, bf16[128,128]{1,0:T(8,128)(2,1)}, u32[]{:S(2)}) copy-start(bf16[128,128]{1,0:T(8,128)(2,1)} %param.7) | copy-start | bytes 98308
  7.2 240.0 %all-reduce.2.cloned.1.call-start = ((), (), s32[]{:S(2)}) async-start(), calls=%async_computation | async-start | bytes 131072 | tf_op jit(solution)/shard_map/psum | solution.py:44
  7.2 21.3 %collective-permute-start.3 = (bf16[1024,128]{1,0:T(8,128)(2,1)}, bf16[1024,128]{1,0:T(8,128)(2,1)S(1)}, u32[]{:S(2)}, u32[]{:S(2)}) collective-permute-start(bf16[1024,128]{1,0:T(8,128)(2,1)} %param.4), channel_id=1, source_target_pairs={{2,0},{3,1},{4,2},{5,3},{6,4},{7,5},{8,6},{9,7},{10,8},{11,9},{12,... | collective-permute-start | bytes 786440 | tf_op jit(solution)/shard_map/ppermute | solution.py:13
  8.5 19.9 %collective-permute-start.2 = (bf16[1024,128]{1,0:T(8,128)(2,1)}, bf16[1024,128]{1,0:T(8,128)(2,1)S(1)}, u32[]{:S(2)}, u32[]{:S(2)}) collective-permute-start(bf16[1024,128]{1,0:T(8,128)(2,1)} %param.4), channel_id=1, source_target_pairs={{1,0},{2,1},{3,2},{4,3},{5,4},{6,5},{7,6},{8,7},{9,8},{10,9},{11,1... | collective-permute-start | bytes 786440 | tf_op jit(solution)/shard_map/ppermute | solution.py:13
  9.8 17.6 %collective-permute-start.1 = (bf16[1024,128]{1,0:T(8,128)(2,1)}, bf16[1024,128]{1,0:T(8,128)(2,1)S(1)}, u32[]{:S(2)}, u32[]{:S(2)}) collective-permute-start(bf16[1024,128]{1,0:T(8,128)(2,1)} %param.4), channel_id=1, source_target_pairs={{0,1},{1,2},{2,3},{3,4},{4,5},{5,6},{6,7},{7,8},{8,9},{9,10},{10,1... | collective-permute-start | bytes 786440 | tf_op jit(solution)/shard_map/ppermute | solution.py:13
  12.9 14.5 %collective-permute-start = (bf16[1024,128]{1,0:T(8,128)(2,1)}, bf16[1024,128]{1,0:T(8,128)(2,1)S(1)}, u32[]{:S(2)}, u32[]{:S(2)}) collective-permute-start(bf16[1024,128]{1,0:T(8,128)(2,1)} %param.4), channel_id=1, source_target_pairs={{0,2},{1,3},{2,4},{3,5},{4,6},{5,7},{6,8},{7,9},{8,10},{9,11},{10,... | collective-permute-start | bytes 786440 | tf_op jit(solution)/shard_map/ppermute | solution.py:13
  45.3 11.1 %collective-permute-start.4 = (bf16[1024,128]{1,0:T(8,128)(2,1)S(1)}, bf16[1024,128]{1,0:T(8,128)(2,1)S(1)}, u32[]{:S(2)}, u32[]{:S(2)}) collective-permute-start(bf16[1024,128]{1,0:T(8,128)(2,1)S(1)} %bitcast.67), channel_id=1, source_target_pairs={{0,2},{1,3},{2,4},{3,5},{4,6},{5,7},{6,8},{7,9},{8,10},{9,11},{10,... | collective-permute-start | bytes 786440 | tf_op jit(solution)/shard_map/ppermute | solution.py:13
  49.5 6.9 %collective-permute-start.5 = (bf16[1024,128]{1,0:T(8,128)(2,1)S(1)}, bf16[1024,128]{1,0:T(8,128)(2,1)S(1)}, u32[]{:S(2)}, u32[]{:S(2)}) collective-permute-start(bf16[1024,128]{1,0:T(8,128)(2,1)S(1)} %bitcast.68), channel_id=1, source_target_pairs={{0,1},{1,2},{2,3},{3,4},{4,5},{5,6},{6,7},{7,8},{8,9},{9,10},{10,1... | collective-permute-start | bytes 786440 | tf_op jit(solution)/shard_map/ppermute | solution.py:13
  53.8 10.1 %collective-permute-start.7 = (bf16[1024,128]{1,0:T(8,128)(2,1)S(1)}, bf16[1024,128]{1,0:T(8,128)(2,1)S(1)}, u32[]{:S(2)}, u32[]{:S(2)}) collective-permute-start(bf16[1024,128]{1,0:T(8,128)(2,1)S(1)} %bitcast.69), channel_id=1, source_target_pairs={{2,0},{3,1},{4,2},{5,3},{6,4},{7,5},{8,6},{9,7},{10,8},{11,9},{12,... | collective-permute-start | bytes 786440 | tf_op jit(solution)/shard_map/ppermute | solution.py:13
  55.1 3.4 %collective-permute-start.6 = (bf16[1024,128]{1,0:T(8,128)(2,1)S(1)}, bf16[1024,128]{1,0:T(8,128)(2,1)S(1)}, u32[]{:S(2)}, u32[]{:S(2)}) collective-permute-start(bf16[1024,128]{1,0:T(8,128)(2,1)S(1)} %bitcast.70), channel_id=1, source_target_pairs={{1,0},{2,1},{3,2},{4,3},{5,4},{6,5},{7,6},{8,7},{9,8},{10,9},{11,1... | collective-permute-start | bytes 786440 | tf_op jit(solution)/shard_map/ppermute | solution.py:13
  72.5 8.2 %copy-start.1 = (bf16[1024,128]{1,0:T(8,128)(2,1)S(1)}, bf16[1024,128]{1,0:T(8,128)(2,1)}, u32[]{:S(2)}) copy-start(bf16[1024,128]{1,0:T(8,128)(2,1)} %param.4) | copy-start | bytes 786436
  80.8 14.1 %collective-permute-start.8 = (bf16[1024,128]{1,0:T(8,128)(2,1)S(1)}, bf16[1024,128]{1,0:T(8,128)(2,1)S(1)}, u32[]{:S(2)}, u32[]{:S(2)}) collective-permute-start(bf16[1024,128]{1,0:T(8,128)(2,1)S(1)} %fusion.42), channel_id=1, source_target_pairs={{0,2},{1,3},{2,4},{3,5},{4,6},{5,7},{6,8},{7,9},{8,10},{9,11},{10,... | collective-permute-start | bytes 786440 | tf_op jit(solution)/shard_map/ppermute | solution.py:13
  88.8 6.0 %collective-permute-start.9 = (bf16[1024,128]{1,0:T(8,128)(2,1)S(1)}, bf16[1024,128]{1,0:T(8,128)(2,1)S(1)}, u32[]{:S(2)}, u32[]{:S(2)}) collective-permute-start(bf16[1024,128]{1,0:T(8,128)(2,1)S(1)} %fusion.42), channel_id=1, source_target_pairs={{0,1},{1,2},{2,3},{3,4},{4,5},{5,6},{6,7},{7,8},{8,9},{9,10},{10,1... | collective-permute-start | bytes 786440 | tf_op jit(solution)/shard_map/ppermute | solution.py:13
  90.1 11.5 %collective-permute-start.11 = (bf16[1024,128]{1,0:T(8,128)(2,1)S(1)}, bf16[1024,128]{1,0:T(8,128)(2,1)S(1)}, u32[]{:S(2)}, u32[]{:S(2)}) collective-permute-start(bf16[1024,128]{1,0:T(8,128)(2,1)S(1)} %fusion.42), channel_id=1, source_target_pairs={{2,0},{3,1},{4,2},{5,3},{6,4},{7,5},{8,6},{9,7},{10,8},{11,9},{12,... | collective-permute-start | bytes 786440 | tf_op jit(solution)/shard_map/ppermute | solution.py:13
  91.4 3.6 %collective-permute-start.10 = (bf16[1024,128]{1,0:T(8,128)(2,1)S(1)}, bf16[1024,128]{1,0:T(8,128)(2,1)S(1)}, u32[]{:S(2)}, u32[]{:S(2)}) collective-permute-start(bf16[1024,128]{1,0:T(8,128)(2,1)S(1)} %fusion.42), channel_id=1, source_target_pairs={{1,0},{2,1},{3,2},{4,3},{5,4},{6,5},{7,6},{8,7},{9,8},{10,9},{11,1... | collective-permute-start | bytes 786440 | tf_op jit(solution)/shard_map/ppermute | solution.py:13
  118.5 12.1 %collective-permute-start.12 = (bf16[1024,128]{1,0:T(8,128)(2,1)S(1)}, bf16[1024,128]{1,0:T(8,128)(2,1)S(1)}, u32[]{:S(2)}, u32[]{:S(2)}) collective-permute-start(bf16[1024,128]{1,0:T(8,128)(2,1)S(1)} %fusion.41), channel_id=1, source_target_pairs={{0,2},{1,3},{2,4},{3,5},{4,6},{5,7},{6,8},{7,9},{8,10},{9,11},{10,... | collective-permute-start | bytes 786440 | tf_op jit(solution)/shard_map/ppermute | solution.py:13
  123.5 7.2 %collective-permute-start.13 = (bf16[1024,128]{1,0:T(8,128)(2,1)S(1)}, bf16[1024,128]{1,0:T(8,128)(2,1)S(1)}, u32[]{:S(2)}, u32[]{:S(2)}) collective-permute-start(bf16[1024,128]{1,0:T(8,128)(2,1)S(1)} %fusion.41), channel_id=1, source_target_pairs={{0,1},{1,2},{2,3},{3,4},{4,5},{5,6},{6,7},{7,8},{8,9},{9,10},{10,1... | collective-permute-start | bytes 786440 | tf_op jit(solution)/shard_map/ppermute | solution.py:13
  128.0 10.6 %collective-permute-start.15 = (bf16[1024,128]{1,0:T(8,128)(2,1)S(1)}, bf16[1024,128]{1,0:T(8,128)(2,1)S(1)}, u32[]{:S(2)}, u32[]{:S(2)}) collective-permute-start(bf16[1024,128]{1,0:T(8,128)(2,1)S(1)} %fusion.41), channel_id=1, source_target_pairs={{2,0},{3,1},{4,2},{5,3},{6,4},{7,5},{8,6},{9,7},{10,8},{11,9},{12,... | collective-permute-start | bytes 786440 | tf_op jit(solution)/shard_map/ppermute | solution.py:13
  129.3 3.4 %collective-permute-start.14 = (bf16[1024,128]{1,0:T(8,128)(2,1)S(1)}, bf16[1024,128]{1,0:T(8,128)(2,1)S(1)}, u32[]{:S(2)}, u32[]{:S(2)}) collective-permute-start(bf16[1024,128]{1,0:T(8,128)(2,1)S(1)} %fusion.41), channel_id=1, source_target_pairs={{1,0},{2,1},{3,2},{4,3},{5,4},{6,5},{7,6},{8,7},{9,8},{10,9},{11,1... | collective-permute-start | bytes 786440 | tf_op jit(solution)/shard_map/ppermute | solution.py:13
Sparse Core Ops, SparseCore 0:
  156.5 90.6 all-reduce.1
where the time goes:
time: 257 us; the launch traced here: 256 us
  waiting for transfers between devices  121 us (47%)
  starting transfers between devices  46.4 us (18%)
  local copies, waits for them, and re-layouts  35.9 us (14%)
  matrix products  34.6 us (13%)
  between operations  14.4 us (6%)
  other arithmetic  3.04 us (1%)
    psum x1, waiting for transfers between devices, body(): total = lax.psum(partial_gram, 'row')  89.9 us
    ppermute x16, starting transfers between devices, shifted(): return lax.ppermute(block, axis, route)  46.3 us
    gather x4, local copies, waits for them, and re-layouts, apply_operator(): picked = blocks[position]  34.2 us
    dot_general x4, matrix products, apply_operator(): jnp.einsum('rjab,rjbk->rak', grouped, picked, preferred_element_type=jnp....  32.7 us
    ppermute x16, waiting for transfers between devices, shifted(): return lax.ppermute(block, axis, route)  31.3 us
  transfers between devices with their start and end apart: 17, of which 9 were waited for; matrix products, arithmetic and copies ran while one was open for 1% of the time, Pallas kernels for 0%

commit v1 on v0

v1 whole, which is shorter than its diff:
```python
import functools

import jax
import jax.numpy as jnp
from jax import lax
from jax.experimental import pallas as pl
from jax.experimental.pallas import tpu as pltpu
from jax.sharding import PartitionSpec as P

REACH = 2
DEG = 4
CHUNK = 1
OWN, SIB, PAR, OTH, EXT = range(5)


def kernel(nrow, per_row, vec, tiles_hbm, cols, ritz, rot, gram, e0, e1, e2, e3, tiles, pos, fil, part, rs, tot, gath,
           tile_sem, own_sem, send_sem, recv_sem, g_send, g_recv, a_send, a_recv):
    ext = (e0, e1, e2, e3)
    tr, tile, width = vec.shape
    nch = tr // CHUNK
    zero_block = 5 * tr
    me = lax.axis_index("row")
    core = lax.rem(me, 2)
    chip = lax.div(me, 2)
    odd = lax.rem(chip, 2)
    sign = 1 - 2 * odd
    near = 1 - odd
    is_near = core == near
    sib = me + 1 - 2 * core
    partner = me + 2 * sign
    ahead = me + 4 * sign
    behind = me - 4 * sign
    has_ahead = jnp.logical_and(ahead >= 0, ahead < nrow)
    has_behind = jnp.logical_and(behind >= 0, behind < nrow)

    own_copy = pltpu.make_async_copy(vec, e0.at[pl.ds(0, tr)], own_sem)
    own_copy.start()

    def tile_copy(t):
        rows = pl.ds(t * per_row, per_row)
        return pltpu.make_async_copy(tiles_hbm.at[rows], tiles.at[rows], tile_sem.at[t])

    barrier = pltpu.get_barrier_semaphore()

    def greet(d, _):
        pl.semaphore_signal(barrier, inc=1, device_id={"row": lax.rem(me + d, nrow)}, device_id_type=pl.DeviceIdType.MESH)
        return 0

    lax.fori_loop(1, nrow, greet, 0)
    pl.semaphore_wait(barrier, nrow - 1)

    def send(k, kind, ch, src=None):
        buf = ext[k]
        at = ch * CHUNK
        origin, place, target = (
            (OWN, SIB, sib),
            (OWN, PAR, partner),
            (PAR, OTH, ahead),
            (PAR + is_near.astype(jnp.int32), EXT, sib),
        )[kind]
        source = buf.at[pl.ds(origin * tr + at, CHUNK)] if src is None else src.at[pl.ds(at, CHUNK)]
        return pltpu.make_async_remote_copy(
            src_ref=source,
            dst_ref=buf.at[pl.ds(place * tr + at, CHUNK)],
            send_sem=send_sem.at[k, kind, ch],
            recv_sem=recv_sem.at[k, kind, ch],
            device_id={"row": target},
            device_id_type=pl.DeviceIdType.MESH,
        )

    def send_own(k, ch, src=None):
        send(k, 1, ch, src).start()
        send(k, 0, ch, src).start()

    def forward_partner(k, ch):
        send(k, 1, ch).wait_recv()

        @pl.when(has_ahead)
        def _():
            send(k, 2, ch).start()

        @pl.when(jnp.logical_not(is_near))
        def _():
            send(k, 3, ch).start()

    def forward_other(k, ch):
        @pl.when(has_behind)
        def _():
            send(k, 2, ch).wait_recv()

            @pl.when(is_near)
            def _():
                send(k, 3, ch).start()

    def forward_all(k):
        forward_partner(k, 0)

        def one(ch, _):
            forward_partner(k, ch)
            forward_other(k, ch - 1)
            return 0

        lax.fori_loop(1, nch, one, 0)
        forward_other(k, nch - 1)

        def rest(ch, _):
            send(k, 0, ch).wait_recv()

            @pl.when(jnp.logical_or(is_near, has_behind))
            def _():
                send(k, 3, ch).wait_recv()

            return 0

        lax.fori_loop(0, nch, rest, 0)

    for ch in range(nch):
        send_own(0, ch, vec)
    for t in range(tr):
        tile_copy(t).start()
    for buf in ext:
        buf[zero_block] = jnp.zeros((tile, width), buf.dtype)

    first_col = (me - REACH) * tr

    def place_of(i, _):
        col = cols[i]
        rel = jnp.where(col >= 0, col - first_col, 0)
        owner = me - REACH + lax.div(rel, tr)
        slot = jnp.where(
            owner == me, OWN,
            jnp.where(owner == sib, SIB, jnp.where(owner == partner, PAR, jnp.where(owner == me - 2 * sign, OTH, EXT))),
        )
        pos[i] = jnp.where(col >= 0, slot * tr + lax.rem(rel, tr), zero_block)
        return 0

    lax.fori_loop(0, tr * per_row, place_of, 0)

    own_copy.wait()
    part[...] = jnp.zeros_like(part)
    for k in range(DEG):
        forward_all(k)
        buf = ext[k]

        def one_row(t, _):
            if k == 0:
                tile_copy(t).wait()
            lhs = jnp.concatenate([tiles[t * per_row + j] for j in range(per_row)], axis=1)
            rhs = jnp.concatenate([buf[pos[t * per_row + j]] for j in range(per_row)], axis=0)
            acc = jnp.dot(lhs, rhs, preferred_element_type=jnp.float32)
            if k > 0:
                acc = 2.0 * acc - ext[k - 1][t].astype(jnp.float32)
            y = acc.astype(jnp.bfloat16)
            if k < DEG - 1:
                ext[k + 1][t] = y
                if CHUNK == 1:
                    send_own(k + 1, t)
                else:
                    @pl.when(lax.rem(t, CHUNK) == CHUNK - 1)
                    def _():
                        send_own(k + 1, lax.div(t, CHUNK))
            else:
                fil[t] = y
                part[...] += lax.dot_general(y, y, (((0,), (0,)), ((), ())), preferred_element_type=jnp.float32).reshape(part.shape)
            return 0

        lax.fori_loop(0, tr, one_row, 0)

    def scatter(d):
        target = lax.rem(me + d, nrow)
        return pltpu.make_async_remote_copy(
            src_ref=part.at[target], dst_ref=rs.at[d], send_sem=g_send.at[d], recv_sem=g_recv.at[d],
            device_id={"row": target}, device_id_type=pl.DeviceIdType.MESH)

    def spread(d):
        target = lax.rem(me + d, nrow)
        return pltpu.make_async_remote_copy(
            src_ref=tot, dst_ref=gath.at[me], send_sem=a_send.at[d], recv_sem=a_recv.at[d],
            device_id={"row": target}, device_id_type=pl.DeviceIdType.MESH)

    for d in range(1, nrow):
        scatter(d).start()

    def rotate(t, _):
        rot[t] = jnp.dot(fil[t], ritz[...], preferred_element_type=jnp.float32).astype(rot.dtype)
        return 0

    lax.fori_loop(0, tr, rotate, 0)
    total = part[me]
    for d in range(1, nrow):
        scatter(d).wait_recv()
        total = total + rs[d]
    total = total * float(nrow * tr * tile) ** (-0.5)
    tot[...] = total
    for d in range(1, nrow):
        spread(d).start()
    gath[me] = total
    for k in range(DEG):
        def drain(ch, _):
            send(k, 0, ch).wait_send()
            send(k, 1, ch).wait_send()

            @pl.when(has_ahead)
            def _():
                send(k, 2, ch).wait_send()

            @pl.when(jnp.logical_or(jnp.logical_not(is_near), has_behind))
            def _():
                send(k, 3, ch).wait_send()

            return 0

        lax.fori_loop(0, nch, drain, 0)
    for d in range(1, nrow):
        scatter(d).wait_send()
    for d in range(1, nrow):
        spread(d).wait_recv()
        spread(d).wait_send()
    gram[...] = gath[...]


def body(vectors, tiles, tile_cols, ritz):
    rows_here, width = vectors.shape
    tile = tiles.shape[1]
    tr = rows_here // tile
    per_row = tiles.shape[0] // tr
    nrow = lax.axis_size("row")
    nch = tr // CHUNK
    share = (nrow, width // nrow, width)
    vmem = pl.BlockSpec(memory_space=pltpu.VMEM)
    ext = pltpu.VMEM((5 * tr + 1, tile, width), jnp.bfloat16)
    rot, gram = pl.pallas_call(
        functools.partial(kernel, nrow, per_row),
        out_shape=(
            jax.ShapeDtypeStruct((tr, tile, width), jnp.bfloat16),
            jax.ShapeDtypeStruct(share, jnp.float32),
        ),
        in_specs=[
            pl.BlockSpec(memory_space=pl.ANY),
            pl.BlockSpec(memory_space=pl.ANY),
            pl.BlockSpec(memory_space=pltpu.SMEM),
            vmem,
        ],
        out_specs=(vmem, vmem),
        scratch_shapes=[
            ext, ext, ext, ext,
            pltpu.VMEM(tiles.shape, jnp.bfloat16),
            pltpu.SMEM((tr * per_row,), jnp.int32),
            pltpu.VMEM((tr, tile, width), jnp.bfloat16),
            pltpu.VMEM(share, jnp.float32),
            pltpu.VMEM(share, jnp.float32),
            pltpu.VMEM(share[1:], jnp.float32),
            pltpu.VMEM(share, jnp.float32),
            pltpu.SemaphoreType.DMA((tr,)),
            pltpu.SemaphoreType.DMA,
            pltpu.SemaphoreType.DMA((DEG, 4, nch)),
            pltpu.SemaphoreType.DMA((DEG, 4, nch)),
            pltpu.SemaphoreType.DMA((nrow,)),
            pltpu.SemaphoreType.DMA((nrow,)),
            pltpu.SemaphoreType.DMA((nrow,)),
            pltpu.SemaphoreType.DMA((nrow,)),
        ],
        compiler_params=pltpu.CompilerParams(
            collective_id=0, has_side_effects=True, vmem_limit_bytes=56 * 2**20
        ),
        cost_estimate=pl.CostEstimate(
            flops=2 * DEG * tiles.size * width, bytes_accessed=2 * tiles.size, transcendentals=0
        ),
    )(vectors.reshape(tr, tile, width), tiles, tile_cols, ritz)
    return rot.reshape(rows_here, width), gram.reshape(width, width)


def solution(mesh):
    return jax.shard_map(
        body,
        mesh=mesh,
        in_specs=(
            P(("parts", "row"), None),
            P(("parts", "row"), None, None),
            P(("parts", "row")),
            P("parts", None),
        ),
        out_specs=(P(("parts", "row"), None), P("parts", None)),
        check_vma=False,
    )
```

time: 257 us -> 86.6 us (0.34)
  waiting for transfers between devices: 121 us -> 0 us
  Pallas kernels: 0 us -> 82.5 us
  starting transfers between devices: 46.4 us -> 0 us
  matrix products: 34.6 us -> 0 us
  local copies, waits for them, and re-layouts: 35.9 us -> 3.14 us
  between operations: 14.4 us -> 0.64 us
  other arithmetic: 3.04 us -> 0 us
    psum x1 -> x0, waiting for transfers between devices: 89.9 us -> none  [body(): total = lax.psum(partial_gram, 'row')]
    pallas_call x0 -> x1, Pallas kernels: none -> 82.5 us  [body(): pl.pallas_call(functools.partial(kernel, nrow, per_row), out_shape=(jax.S...]
    ppermute x16 -> x0, starting transfers between devices: 46.3 us -> none  [shifted(): return lax.ppermute(block, axis, route)]
    dot_general x6 -> x0, matrix products: 34.6 us -> none  [the longest x4 32.7 us: apply_operator(): jnp.einsum('rjab,rjbk->rak', grouped, picked, preferred_element_type=jnp....]
    gather x4 -> x0, local copies, waits for them, and re-layouts: 34.2 us -> none  [apply_operator(): picked = blocks[position]]
    ppermute x16 -> x0, waiting for transfers between devices: 31.3 us -> none  [shifted(): return lax.ppermute(block, axis, route)]
  transfers between devices with their start and end apart: 17 -> 0, of which waited for: 9 -> 0; matrix products, arithmetic and copies ran while one was open for 1% -> 0% of each run, Pallas kernels for 0% -> 0%
where the time goes in v1:
time: 86.6 us; the launch traced here: 86.3 us
  Pallas kernels  82.5 us (95%)
  local copies, waits for them, and re-layouts  3.14 us (4%)
    pallas_call x1, Pallas kernels, body(): pl.pallas_call(functools.partial(kernel, nrow, per_row), out_shape=(jax.S...  82.5 us
    unnamed x2, local copies, waits for them, and re-layouts  3.14 us

profile of v1, /device:TPU:0, one launch (start us, length us, event | category | flops | bytes accessed | tf_op | source)
XLA Modules:
  0.0 86.3 jit_solution(16515420349662814299)
XLA Ops:
  0.6 82.5 %shard_map.59 = (bf16[8,128,128]{2,1,0:T(8,128)(2,1)}, f32[16,8,128]{2,1,0:T(8,128)}) custom-call(bf16[8,128,128]{2,1,0:T(8,128)(2,1)} %bitcast.5, bf16[256,128,128]{2,1,0:T(8,128)(2,1)} %tiles_hbm.1, s32[256]{0:T(256)} %cols.1, bf16[128,128]{1,0:T(8,128)(2,1)} %ritz.1), custom_call_target="tpu_custom_call" | custom-call | flops 4294967296 | bytes 8388608 | tf_op jit(solution)/shard_map/pallas_call | solution.py:232
  83.2 1.7 %copy.8 = bf16[1024,128]{1,0:T(8,128)(2,1)} copy(bf16[1024,128]{1,0:T(8,128)(2,1)} %bitcast.3) | data formatting | bytes 524288
  84.8 1.5 %copy.9 = f32[128,128]{1,0:T(8,128)} copy(f32[128,128]{1,0:T(8,128)} %bitcast.4) | data formatting | bytes 131072

commit v2 on v1

--- a/solution.py
+++ b/solution.py
@@ -10,10 +10,13 @@
 REACH = 2
 DEG = 4
 CHUNK = 1
+PARTNER_LAG = 4
+OTHER_LAG = 8
+DIRECT = 1
 OWN, SIB, PAR, OTH, EXT = range(5)
 
 
-def kernel(nrow, per_row, vec, tiles_hbm, cols, ritz, rot, gram, e0, e1, e2, e3, tiles, pos, fil, part, rs, tot, gath,
+def kernel(nrow, per_row, vec, tiles_hbm, cols, ritz, rot, gram, e0, e1, e2, e3, tiles, table, pos, fil, part, rs, tot, gath,
            tile_sem, own_sem, send_sem, recv_sem, g_send, g_recv, a_send, a_recv):
     ext = (e0, e1, e2, e3)
     tr, tile, width = vec.shape
@@ -30,6 +33,7 @@
     partner = me + 2 * sign
     ahead = me + 4 * sign
     behind = me - 4 * sign
+    far = ahead + 1 - 2 * core
     has_ahead = jnp.logical_and(ahead >= 0, ahead < nrow)
     has_behind = jnp.logical_and(behind >= 0, behind < nrow)
 
@@ -57,13 +61,14 @@
             (OWN, PAR, partner),
             (PAR, OTH, ahead),
             (PAR + is_near.astype(jnp.int32), EXT, sib),
+            (PAR, EXT, far),
         )[kind]
         source = buf.at[pl.ds(origin * tr + at, CHUNK)] if src is None else src.at[pl.ds(at, CHUNK)]
         return pltpu.make_async_remote_copy(
             src_ref=source,
             dst_ref=buf.at[pl.ds(place * tr + at, CHUNK)],
             send_sem=send_sem.at[k, kind, ch],
-            recv_sem=recv_sem.at[k, kind, ch],
+            recv_sem=recv_sem.at[k, min(kind, 3), ch],
             device_id={"row": target},
             device_id_type=pl.DeviceIdType.MESH,
         )
@@ -79,6 +84,10 @@
         def _():
             send(k, 2, ch).start()
 
+            @pl.when(jnp.logical_and(is_near, ch >= nch - DIRECT))
+            def _():
+                send(k, 4, ch).start()
+
         @pl.when(jnp.logical_not(is_near))
         def _():
             send(k, 3, ch).start()
@@ -88,20 +97,31 @@
         def _():
             send(k, 2, ch).wait_recv()
 
-            @pl.when(is_near)
+            @pl.when(jnp.logical_and(is_near, ch < nch - DIRECT))
             def _():
                 send(k, 3, ch).start()
 
-    def forward_all(k):
-        forward_partner(k, 0)
-
-        def one(ch, _):
-            forward_partner(k, ch)
-            forward_other(k, ch - 1)
+    def relay(k, step):
+        to_partner = step - PARTNER_LAG
+        to_other = step - OTHER_LAG
+
+        @pl.when(jnp.logical_and(to_partner >= 0, to_partner < nch))
+        def _():
+            forward_partner(k, to_partner)
+
+        @pl.when(jnp.logical_and(to_other >= 0, to_other < nch))
+        def _():
+            forward_other(k, to_other)
+
+    def with_relay(k, work):
+        def one(step, _):
+            work(step)
+            relay(k, step)
             return 0
 
-        lax.fori_loop(1, nch, one, 0)
-        forward_other(k, nch - 1)
+        def tail(step, _):
+            relay(k, step)
+            return 0
 
         def rest(ch, _):
             send(k, 0, ch).wait_recv()
@@ -112,6 +132,8 @@
 
             return 0
 
+        lax.fori_loop(0, nch, one, 0)
+        lax.fori_loop(nch, nch + OTHER_LAG, tail, 0)
         lax.fori_loop(0, nch, rest, 0)
 
     for ch in range(nch):
@@ -123,48 +145,54 @@
 
     first_col = (me - REACH) * tr
 
-    def place_of(i, _):
-        col = cols[i]
-        rel = jnp.where(col >= 0, col - first_col, 0)
-        owner = me - REACH + lax.div(rel, tr)
+    for r in range(2 * REACH + 1):
+        owner = me - REACH + r
         slot = jnp.where(
             owner == me, OWN,
             jnp.where(owner == sib, SIB, jnp.where(owner == partner, PAR, jnp.where(owner == me - 2 * sign, OTH, EXT))),
         )
-        pos[i] = jnp.where(col >= 0, slot * tr + lax.rem(rel, tr), zero_block)
-        return 0
-
-    lax.fori_loop(0, tr * per_row, place_of, 0)
-
+        for b in range(tr):
+            table[r * tr + b] = slot * tr + b
+    table[zero_block] = zero_block
+
+    def place_of(i):
+        col = cols[i]
+        pos[i] = table[jnp.where(col >= 0, jnp.clip(col - first_col, 0, zero_block), zero_block)]
+
+    share_of = CHUNK * per_row
+    part[...] = jnp.zeros_like(part)
+    with_relay(0, lambda step: [place_of(step * share_of + j) for j in range(share_of)])
     own_copy.wait()
-    part[...] = jnp.zeros_like(part)
     for k in range(DEG):
-        forward_all(k)
         buf = ext[k]
 
-        def one_row(t, _):
-            if k == 0:
-                tile_copy(t).wait()
-            lhs = jnp.concatenate([tiles[t * per_row + j] for j in range(per_row)], axis=1)
-            rhs = jnp.concatenate([buf[pos[t * per_row + j]] for j in range(per_row)], axis=0)
-            acc = jnp.dot(lhs, rhs, preferred_element_type=jnp.float32)
-            if k > 0:
-                acc = 2.0 * acc - ext[k - 1][t].astype(jnp.float32)
-            y = acc.astype(jnp.bfloat16)
+        def rows_of(ch):
+            for r in range(CHUNK):
+                t = ch * CHUNK + r
+                if k == 0:
+                    tile_copy(t).wait()
+                lhs = jnp.concatenate([tiles[t * per_row + j] for j in range(per_row)], axis=1)
+                rhs = jnp.concatenate([buf[pos[t * per_row + j]] for j in range(per_row)], axis=0)
+                acc = jnp.dot(lhs, rhs, preferred_element_type=jnp.float32)
+                if k > 0:
+                    acc = 2.0 * acc - ext[k - 1][t].astype(jnp.float32)
+                y = acc.astype(jnp.bfloat16)
+                if k < DEG - 1:
+                    ext[k + 1][t] = y
+                else:
+                    fil[t] = y
+                    part[...] += lax.dot_general(y, y, (((0,), (0,)), ((), ())), preferred_element_type=jnp.float32).reshape(part.shape)
             if k < DEG - 1:
-                ext[k + 1][t] = y
-                if CHUNK == 1:
-                    send_own(k + 1, t)
-                else:
-                    @pl.when(lax.rem(t, CHUNK) == CHUNK - 1)
-                    def _():
-                        send_own(k + 1, lax.div(t, CHUNK))
-            else:
-                fil[t] = y
-                part[...] += lax.dot_general(y, y, (((0,), (0,)), ((), ())), preferred_element_type=jnp.float32).reshape(part.shape)
-            return 0
-
-        lax.fori_loop(0, tr, one_row, 0)
+                send_own(k + 1, ch)
+
+        if k < DEG - 1:
+            with_relay(k + 1, rows_of)
+        else:
+            def last(ch, _):
+                rows_of(ch)
+                return 0
+
+            lax.fori_loop(0, nch, last, 0)
 
     def scatter(d):
         target = lax.rem(me + d, nrow)
@@ -204,7 +232,11 @@
             def _():
                 send(k, 2, ch).wait_send()
 
-            @pl.when(jnp.logical_or(jnp.logical_not(is_near), has_behind))
+                @pl.when(jnp.logical_and(is_near, ch >= nch - DIRECT))
+                def _():
+                    send(k, 4, ch).wait_send()
+
+            @pl.when(jnp.logical_or(jnp.logical_not(is_near), jnp.logical_and(has_behind, ch < nch - DIRECT)))
             def _():
                 send(k, 3, ch).wait_send()
 
@@ -245,6 +277,7 @@
         scratch_shapes=[
             ext, ext, ext, ext,
             pltpu.VMEM(tiles.shape, jnp.bfloat16),
+            pltpu.SMEM((5 * tr + 1,), jnp.int32),
             pltpu.SMEM((tr * per_row,), jnp.int32),
             pltpu.VMEM((tr, tile, width), jnp.bfloat16),
             pltpu.VMEM(share, jnp.float32),
@@ -253,7 +286,7 @@
             pltpu.VMEM(share, jnp.float32),
             pltpu.SemaphoreType.DMA((tr,)),
             pltpu.SemaphoreType.DMA,
-            pltpu.SemaphoreType.DMA((DEG, 4, nch)),
+            pltpu.SemaphoreType.DMA((DEG, 5, nch)),
             pltpu.SemaphoreType.DMA((DEG, 4, nch)),
             pltpu.SemaphoreType.DMA((nrow,)),
             pltpu.SemaphoreType.DMA((nrow,)),

time: 86.6 us -> 71.9 us (0.83)
  Pallas kernels: 82.5 us -> 67.9 us
    pallas_call x1, Pallas kernels: 82.5 us -> 67.9 us  [body(): pl.pallas_call(functools.partial(kernel, nrow, per_row), out_shape=(jax.S...]
where the time goes in v2:
time: 71.9 us; the launch traced here: 71.7 us
  Pallas kernels  67.9 us (94%)
  local copies, waits for them, and re-layouts  3.14 us (4%)
    pallas_call x1, Pallas kernels, body(): pl.pallas_call(functools.partial(kernel, nrow, per_row), out_shape=(jax.S...  67.9 us
    unnamed x2, local copies, waits for them, and re-layouts  3.14 us

profile of v2, /device:TPU:0, one launch (start us, length us, event | category | flops | bytes accessed | tf_op | source)
XLA Modules:
  0.0 71.7 jit_solution(10948331864631546116)
XLA Ops:
  0.6 67.9 %shard_map.59 = (bf16[8,128,128]{2,1,0:T(8,128)(2,1)}, f32[16,8,128]{2,1,0:T(8,128)}) custom-call(bf16[8,128,128]{2,1,0:T(8,128)(2,1)} %bitcast.5, bf16[256,128,128]{2,1,0:T(8,128)(2,1)} %tiles_hbm.1, s32[256]{0:T(256)} %cols.1, bf16[128,128]{1,0:T(8,128)(2,1)} %ritz.1), custom_call_target="tpu_custom_call" | custom-call | flops 4294967296 | bytes 8388608 | tf_op jit(solution)/shard_map/pallas_call | solution.py:264
  68.5 1.7 %copy.8 = bf16[1024,128]{1,0:T(8,128)(2,1)} copy(bf16[1024,128]{1,0:T(8,128)(2,1)} %bitcast.3) | data formatting | bytes 524288
  70.2 1.5 %copy.9 = f32[128,128]{1,0:T(8,128)} copy(f32[128,128]{1,0:T(8,128)} %bitcast.4) | data formatting | bytes 131072

commit v3 on v2

--- a/solution.py
+++ b/solution.py
@@ -17,7 +17,7 @@
 
 
 def kernel(nrow, per_row, vec, tiles_hbm, cols, ritz, rot, gram, e0, e1, e2, e3, tiles, table, pos, fil, part, rs, tot, gath,
-           tile_sem, own_sem, send_sem, recv_sem, g_send, g_recv, a_send, a_recv):
+           tile_sem, own_sem, send_sem, recv_sem, whole_sem, g_send, g_recv, a_send, a_recv):
     ext = (e0, e1, e2, e3)
     tr, tile, width = vec.shape
     nch = tr // CHUNK
@@ -53,7 +53,7 @@
     lax.fori_loop(1, nrow, greet, 0)
     pl.semaphore_wait(barrier, nrow - 1)
 
-    def send(k, kind, ch, src=None):
+    def send(k, kind, ch, src=None, count=CHUNK):
         buf = ext[k]
         at = ch * CHUNK
         origin, place, target = (
@@ -63,12 +63,12 @@
             (PAR + is_near.astype(jnp.int32), EXT, sib),
             (PAR, EXT, far),
         )[kind]
-        source = buf.at[pl.ds(origin * tr + at, CHUNK)] if src is None else src.at[pl.ds(at, CHUNK)]
+        source = buf.at[pl.ds(origin * tr + at, count)] if src is None else src.at[pl.ds(at, CHUNK)]
         return pltpu.make_async_remote_copy(
             src_ref=source,
-            dst_ref=buf.at[pl.ds(place * tr + at, CHUNK)],
-            send_sem=send_sem.at[k, kind, ch],
-            recv_sem=recv_sem.at[k, min(kind, 3), ch],
+            dst_ref=buf.at[pl.ds(place * tr + at, count)],
+            send_sem=send_sem.at[k, kind],
+            recv_sem=whole_sem.at[k, min(kind, 3)] if kind in (0, 3, 4) else recv_sem.at[k, kind - 1, ch],
             device_id={"row": target},
             device_id_type=pl.DeviceIdType.MESH,
         )
@@ -123,18 +123,13 @@
             relay(k, step)
             return 0
 
-        def rest(ch, _):
-            send(k, 0, ch).wait_recv()
-
-            @pl.when(jnp.logical_or(is_near, has_behind))
-            def _():
-                send(k, 3, ch).wait_recv()
-
-            return 0
-
         lax.fori_loop(0, nch, one, 0)
         lax.fori_loop(nch, nch + OTHER_LAG, tail, 0)
-        lax.fori_loop(0, nch, rest, 0)
+        send(k, 0, 0, count=tr).wait_recv()
+
+        @pl.when(jnp.logical_or(is_near, has_behind))
+        def _():
+            send(k, 3, 0, count=tr).wait_recv()
 
     for ch in range(nch):
         send_own(0, ch, vec)
@@ -188,11 +183,12 @@
         if k < DEG - 1:
             with_relay(k + 1, rows_of)
         else:
-            def last(ch, _):
-                rows_of(ch)
+            def last(pair, _):
+                rows_of(2 * pair)
+                rows_of(2 * pair + 1)
                 return 0
 
-            lax.fori_loop(0, nch, last, 0)
+            lax.fori_loop(0, nch // 2, last, 0)
 
     def scatter(d):
         target = lax.rem(me + d, nrow)
@@ -224,25 +220,25 @@
         spread(d).start()
     gath[me] = total
     for k in range(DEG):
-        def drain(ch, _):
-            send(k, 0, ch).wait_send()
-            send(k, 1, ch).wait_send()
-
-            @pl.when(has_ahead)
+        send(k, 0, 0, count=tr).wait_send()
+        send(k, 1, 0, count=tr).wait_send()
+
+        @pl.when(has_ahead)
+        def _():
+            send(k, 2, 0, count=tr).wait_send()
+
+            @pl.when(is_near)
             def _():
-                send(k, 2, ch).wait_send()
-
-                @pl.when(jnp.logical_and(is_near, ch >= nch - DIRECT))
-                def _():
-                    send(k, 4, ch).wait_send()
-
-            @pl.when(jnp.logical_or(jnp.logical_not(is_near), jnp.logical_and(has_behind, ch < nch - DIRECT)))
-            def _():
-                send(k, 3, ch).wait_send()
-
-            return 0
-
-        lax.fori_loop(0, nch, drain, 0)
+                send(k, 4, 0, count=DIRECT * CHUNK).wait_send()
+
+        @pl.when(jnp.logical_not(is_near))
+        def _():
+            send(k, 3, 0, count=tr).wait_send()
+
+        @pl.when(jnp.logical_and(is_near, has_behind))
+        def _():
+            send(k, 3, 0, count=tr - DIRECT * CHUNK).wait_send()
+
     for d in range(1, nrow):
         scatter(d).wait_send()
     for d in range(1, nrow):
@@ -286,8 +282,9 @@
             pltpu.VMEM(share, jnp.float32),
             pltpu.SemaphoreType.DMA((tr,)),
             pltpu.SemaphoreType.DMA,
-            pltpu.SemaphoreType.DMA((DEG, 5, nch)),
-            pltpu.SemaphoreType.DMA((DEG, 4, nch)),
+            pltpu.SemaphoreType.DMA((DEG, 5)),
+            pltpu.SemaphoreType.DMA((DEG, 2, nch)),
+            pltpu.SemaphoreType.DMA((DEG, 4)),
             pltpu.SemaphoreType.DMA((nrow,)),
             pltpu.SemaphoreType.DMA((nrow,)),
             pltpu.SemaphoreType.DMA((nrow,)),

time: 71.9 us -> 69.8 us (0.971)
  Pallas kernels: 67.9 us -> 65.7 us
    pallas_call x1, Pallas kernels: 67.9 us -> 65.7 us  [body(): pl.pallas_call(functools.partial(kernel, nrow, per_row), out_shape=(jax.S...]
where the time goes in v3:
time: 69.8 us; the launch traced here: 69.5 us
  Pallas kernels  65.7 us (94%)
  local copies, waits for them, and re-layouts  3.14 us (4%)
    pallas_call x1, Pallas kernels, body(): pl.pallas_call(functools.partial(kernel, nrow, per_row), out_shape=(jax.S...  65.7 us
    unnamed x2, local copies, waits for them, and re-layouts  3.14 us

profile of v3, /device:TPU:0, one launch (start us, length us, event | category | flops | bytes accessed | tf_op | source)
XLA Modules:
  0.0 69.5 jit_solution(3007931208639711925)
XLA Ops:
  0.6 65.7 %shard_map.59 = (bf16[8,128,128]{2,1,0:T(8,128)(2,1)}, f32[16,8,128]{2,1,0:T(8,128)}) custom-call(bf16[8,128,128]{2,1,0:T(8,128)(2,1)} %bitcast.5, bf16[256,128,128]{2,1,0:T(8,128)(2,1)} %tiles_hbm.1, s32[256]{0:T(256)} %cols.1, bf16[128,128]{1,0:T(8,128)(2,1)} %ritz.1), custom_call_target="tpu_custom_call" | custom-call | flops 4294967296 | bytes 8388608 | tf_op jit(solution)/shard_map/pallas_call | solution.py:260
  66.4 1.7 %copy.8 = bf16[1024,128]{1,0:T(8,128)(2,1)} copy(bf16[1024,128]{1,0:T(8,128)(2,1)} %bitcast.3) | data formatting | bytes 524288
  68.0 1.5 %copy.9 = f32[128,128]{1,0:T(8,128)} copy(f32[128,128]{1,0:T(8,128)} %bitcast.4) | data formatting | bytes 131072
